TPU v7x, 256 devices: a whole 4x4x8 slice. The times are simulated.
256 devices in a mesh: group: 16 (over x_lo, z), blk: 16 (over y, x_hi, core).
Axes of the slice: x: 4 (x_hi: 2, x_lo: 2; x = x_hi * 2 + x_lo), y: 4, z: 8, core: 2. Of those that a mesh axis runs over, the one named last changes fastest.
Arguments:
- student: bfloat16 [16384, 1024], P('group'), may hold values from -8 to 8
- teacher: bfloat16 [16384, 1024], P('group'), may hold values from -8 to 8
Outputs:
- student_grad: float32 [16384, 1024], P(('group', 'blk'))
All inputs are finite; a program needn't handle non-finite values.
Results may differ from a plain program's by a relative error of at most 0.0008.
Values may be sent and summed in bfloat16 or wider, within the bound.
A program may use at most 64 MiB of HBM per device.

v0:
```python
import jax
import jax.numpy as jnp
from jax import lax
from jax.sharding import PartitionSpec as P

SCALE_FACTORS = (0.5, 1.0, 2.0, 4.0, 8.0)


def kernel_weights(distance, feature_width):
    summed = jnp.zeros(distance.shape, jnp.float32)
    for factor in SCALE_FACTORS:
        summed = summed + 2.0 / factor * jnp.exp(-distance / (feature_width * factor))
    return summed.astype(jnp.bfloat16)


def squares(values):
    wide = values.astype(jnp.float32)
    return jnp.sum(wide * wide, axis=1)


def cross(left, right):
    return lax.dot_general(
        left, right, (((1,), (1,)), ((), ())), preferred_element_type=jnp.float32
    )


def pair_terms(row_block, row_norm, student_cols, teacher_cols):
    feature_width = row_block.shape[1]
    near_dist = (
        row_norm[:, None] + squares(student_cols)[None, :] - 2.0 * cross(row_block, student_cols)
    )
    far_dist = (
        row_norm[:, None] + squares(teacher_cols)[None, :] - 2.0 * cross(row_block, teacher_cols)
    )
    near_weights = kernel_weights(near_dist, feature_width)
    far_weights = kernel_weights(far_dist, feature_width)
    pulled = jnp.dot(near_weights, student_cols, preferred_element_type=jnp.float32)
    pulled = pulled - jnp.dot(far_weights, teacher_cols, preferred_element_type=jnp.float32)
    mass_diff = jnp.sum(near_weights.astype(jnp.float32), axis=1) - jnp.sum(
        far_weights.astype(jnp.float32), axis=1
    )
    return pulled - mass_diff[:, None] * row_block.astype(jnp.float32)


def local(student, teacher):
    local_rows = student.shape[0]
    share_rows = local_rows // lax.axis_size("blk")
    row_count = lax.axis_size("group") * local_rows
    share_start = lax.axis_index("blk") * share_rows
    student_part = lax.dynamic_slice_in_dim(student, share_start, share_rows, 0)
    teacher_part = lax.dynamic_slice_in_dim(teacher, share_start, share_rows, 0)
    row_norm = squares(student)
    partial_value = pair_terms(
        student,
        row_norm,
        lax.all_gather(student_part, "group", axis=0, tiled=True),
        lax.all_gather(teacher_part, "group", axis=0, tiled=True),
    )
    totals = lax.psum(partial_value, "blk")
    summed = lax.dynamic_slice_in_dim(totals, share_start, share_rows, 0)
    return summed / jnp.float32(row_count)


def solution(mesh):
    in_specs = (P("group", None), P("group", None))
    out_specs = P(("group", "blk"), None)
    return jax.shard_map(local, mesh=mesh, in_specs=in_specs, out_specs=out_specs, check_vma=False)
```

profile of v0, /device:TPU:8, one launch (start us, length us, event | category | flops | bytes accessed | tf_op | source)
XLA Modules:
  0.0 347.5 jit_solution(7898218750637531843)
XLA Ops:
  6.5 0.0 copy-start
  6.5 0.0 all-gather.3.cloned.1.call-start
  6.5 1.7 constant_dynamic-slice_fusion.1
  8.3 0.0 all-gather.3.cloned.1.call-update
  8.3 0.0 all-gather.5.cloned.1.call-start
  8.3 0.0 copy-done
  8.3 0.7 constant_dynamic-slice_fusion
  9.0 0.0 all-gather.5.cloned.1.call-update
  9.0 0.0 all-reduce.2.cloned.1.call-start
  9.1 2.1 fusion
  11.2 72.5 %all-gather.3.cloned.1.call-done = bf16[1024,1024]{1,0:T(8,128)(2,1)} async-done(((bf16[64,1024]{1,0:T(8,128)(2,1)}), bf16[1024,1024]{1,0:T(8,128)(2,1)}) %all-gather.3.cloned.1.call-update) | async-done | bytes 2097168 | tf_op jit(solution)/shard_map/all_gather | solution.py:56
  83.6 2.1 multiply_reduce_fusion.1
  85.7 2.3 broadcast_add_fusion
  88.0 5.3 %copy.4 = f32[1024,1024]{0,1:T(8,128)} copy(f32[1024,1024]{1,0:T(8,128)} %broadcast_add_fusion) | data formatting | bytes 8388608 | tf_op jit(solution)/shard_map/add | solution.py:30
  93.4 60.8 %all-gather.5.cloned.1.call-done = bf16[1024,1024]{1,0:T(8,128)(2,1)} async-done(((bf16[64,1024]{1,0:T(8,128)(2,1)}), bf16[1024,1024]{1,0:T(8,128)(2,1)}) %all-gather.5.cloned.1.call-update) | async-done | bytes 2097168 | tf_op jit(solution)/shard_map/all_gather | solution.py:57
  154.2 2.1 multiply_reduce_fusion
  156.3 6.6 %bitcast_subtract_fusion = f32[1024,1024]{1,0:T(8,128)} fusion(bf16[1024,1024]{1,0:T(8,128)(2,1)} %all-gather.5.cloned.1.call-done, bf16[1024,1024]{1,0:T(8,128)(2,1)} %param.2, f32[1024]{0:T(1024)S(1)} %multiply_reduce_fusion, f32[1024]{0:T(1024)S(1)} %fusion), kind=kOutput, calls=%fused_computation.4 | convolution fusion | flops 2150629376 | bytes 8396800 | tf_op jit(solution)/shard_map/dot_general | solution.py:22
  162.8 5.3 %copy.6 = f32[1024,1024]{0,1:T(8,128)} copy(f32[1024,1024]{1,0:T(8,128)} %bitcast_subtract_fusion) | data formatting | bytes 8388608 | tf_op jit(solution)/shard_map/sub | solution.py:33
  168.2 0.0 copy-start.1
  168.2 0.0 copy-start.2
  168.2 5.2 %convert_reduce_fusion = (f32[1024]{0:T(1024)S(1)}, bf16[1024,1024]{0,1:T(8,128)(2,1)S(1)}) fusion(f32[1024,1024]{0,1:T(8,128)} %copy.6), kind=kLoop, calls=%fused_computation.7 | loop fusion | flops 17824768 | bytes 6295552 | tf_op jit(solution)/shard_map/reduce_sum | solution.py:39
  173.4 0.0 copy-done.1
  173.4 0.0 copy-done.2
  173.5 0.0 copy-done.3
  173.5 6.0 %convert_reduce_fusion.1 = (f32[1024]{0:T(1024)S(1)}, bf16[1024,1024]{0,1:T(8,128)(2,1)S(1)}) fusion(f32[1024,1024]{0,1:T(8,128)S(1)} %copy-done.1, bf16[1024,1024]{1,0:T(8,128)(2,1)S(1)} %copy-done.3, bf16[1024,1024]{1,0:T(8,128)(2,1)S(1)} %copy-done.2), kind=kOutput, calls=%fused_computation.8 | convolution fusion | flops 2167405568 | bytes 10489856 | tf_op jit(solution)/shard_map/dot_general | solution.py:22
  179.5 0.0 copy-start.4
  179.5 2.4 fusion.3
  182.0 0.0 copy-done.4
  182.0 4.8 %fusion.1 = f32[1024,1024]{1,0:T(8,128)} fusion(bf16[1024,1024]{1,0:T(8,128)(2,1)S(1)} %copy-done.2, f32[1024,1024]{1,0:T(8,128)S(1)} %fusion.3, f32[1024]{0:T(1024)S(1)} %sub.22, bf16[1024,1024]{0,1:T(8,128)(2,1)S(1)} %get-tuple-element.6, bf16[1024,1024]{1,0:T(8,128)(2,1)S(1)} %copy-done.4), kind=kOutput, calls=%fused_computation.3 | convolution fusion | flops 2151677952 | bytes 14684160 | tf_op jit(solution)/shard_map/dot_general | solution.py:38
  186.8 0.0 all-reduce.2.cloned.1.call-update
  186.8 152.4 %all-reduce.2.cloned.1.call-done = f32[1024,1024]{1,0:T(8,128)} async-done(((f32[1024,1024]{1,0:T(8,128)}), f32[1024,1024]{1,0:T(8,128)}) %all-reduce.2.cloned.1.call-update) | async-done | bytes 4194320 | tf_op jit(solution)/shard_map/psum | solution.py:59
  339.3 1.7 dynamic-slice_multiply_fusion
  (2 shorter events, 0.0 us)
Async XLA Ops:
  6.5 1.8 copy-start
  6.5 77.1 %all-gather.3.cloned.1.call-start = ((), (), s32[]{:S(2)}) async-start(), calls=%async_computation | async-start | bytes 2228224 | tf_op jit(solution)/shard_map/all_gather | solution.py:56
  8.3 145.9 %all-gather.5.cloned.1.call-start = ((), (), s32[]{:S(2)}) async-start(), calls=%async_computation.1 | async-start | bytes 2228224 | tf_op jit(solution)/shard_map/all_gather | solution.py:57
  9.0 330.2 %all-reduce.2.cloned.1.call-start = ((), (), s32[]{:S(2)}) async-start(), calls=%async_computation.2 | async-start | bytes 8388608 | tf_op jit(solution)/shard_map/psum | solution.py:59
  168.2 5.3 %copy-start.1 = (f32[1024,1024]{0,1:T(8,128)S(1)}, f32[1024,1024]{0,1:T(8,128)}, u32[]{:S(2)}) copy-start(f32[1024,1024]{0,1:T(8,128)} %copy.4) | copy-start | bytes 12582916
  168.2 5.3 %copy-start.2 = (bf16[1024,1024]{1,0:T(8,128)(2,1)S(1)}, bf16[1024,1024]{1,0:T(8,128)(2,1)}, u32[]{:S(2)}) copy-start(bf16[1024,1024]{1,0:T(8,128)(2,1)} %param.2) | copy-start | bytes 6291460
  168.2 5.3 %copy-start.3 = (bf16[1024,1024]{1,0:T(8,128)(2,1)S(1)}, bf16[1024,1024]{1,0:T(8,128)(2,1)}, u32[]{:S(2)}) copy-start(bf16[1024,1024]{1,0:T(8,128)(2,1)} %all-gather.3.cloned.1.call-done) | copy-start | bytes 6291460
  179.5 2.5 copy-start.4
Sparse Core Ops, SparseCore 0:
  9.1 74.4 all-gather.2
  85.4 68.7 all-gather.4
  187.0 152.2 all-reduce.1
where the time goes:
time: 355 us; the launch traced here: 347 us
  waiting for transfers between devices  286 us (81%)
  matrix products  19.9 us (6%)
  other arithmetic  15.4 us (4%)
  between operations  13.2 us (4%)
  local copies, waits for them, and re-layouts  13.1 us (4%)
    psum x1, waiting for transfers between devices, local(): totals = lax.psum(partial_value, 'blk')  152 us
    all_gather x1, waiting for transfers between devices, local(): lax.all_gather(student_part, 'group', axis=0, tiled=True)  72.5 us
    all_gather x1, waiting for transfers between devices, local(): lax.all_gather(teacher_part, 'group', axis=0, tiled=True)  60.8 us
    dot_general x2, matrix products, cross(): lax.dot_general(left, right, (((1,), (1,)), ((), ())), preferred_element_...  12.6 us
  transfers between devices with their start and end apart: 3, of which 3 were waited for; matrix products, arithmetic and copies ran while one was open for 4% of the time, Pallas kernels for 0%

commit v1 on v0

v1 whole, which is shorter than its diff:
```python
import functools
import math

import jax
import jax.numpy as jnp
from jax import lax
from jax.experimental import pallas as pl
from jax.experimental.pallas import tpu as pltpu
from jax.sharding import PartitionSpec as P

X_HI = 2
X_LO = 2
CORES = 2
X = X_HI * X_LO
WIDEST = 8.0

LOW = 0.25 * 2.0 ** -0.125
MID = 0.5 * 2.0 ** -0.25
HIGH = 2.0 ** -0.5


def kernel(student, teacher, out, rows, cols, acc, norm, mass, mate, stage, landed,
           load_sem, z_send, z_recv, x_send, x_recv, mate_send, mate_recv, red_send, red_recv,
           *, groups, blks):
    nz = groups // X_LO
    ny = blks // (X_HI * CORES)
    local_rows, width = rows.shape
    part_rows = cols.shape[3]
    share_rows = local_rows // blks
    block_rows = X_HI * CORES * share_rows
    half_nz = nz // 2

    group = lax.axis_index("group")
    blk = lax.axis_index("blk")
    x_lo, z = group // nz, lax.rem(group, nz)
    y, x_hi, core = blk // (X_HI * CORES), lax.rem(blk // CORES, X_HI), lax.rem(blk, CORES)
    x = x_hi * X_LO + x_lo

    def at_z(step):
        return {"group": x_lo * nz + lax.rem(z + step + nz, nz), "blk": blk}

    def at_x(step):
        to = lax.rem(x + step + X, X)
        return {
            "group": lax.rem(to, X_LO) * nz + z,
            "blk": (y * X_HI + to // X_LO) * CORES + core,
        }

    def at_owner(dy, dx):
        to_y, to_x = lax.rem(y + dy, ny), lax.rem(x_hi + dx, X_HI)
        return {"group": group, "blk": (to_y * X_HI + to_x) * CORES + core}

    sibling = {"group": group, "blk": blk + 1 - 2 * core}
    owners = [(dy, dx) for dy in range(ny) for dx in range(X_HI)]
    sources = (student, teacher)

    def own_part(kind, part):
        quarter = lax.rem(x + part, X)
        start = ((y * X + quarter) * CORES + core) * part_rows
        return sources[kind].at[pl.ds(pl.multiple_of(start, part_rows), part_rows)]

    def slot_of(way, dist):
        if dist == 0:
            return 0
        if dist == half_nz:
            return nz - 1
        return dist if way == 0 else half_nz - 1 + dist

    def z_copy(way, dist, kind, part):
        src = own_part(kind, part) if dist == 1 else cols.at[slot_of(way, dist - 1), kind, part]
        return pltpu.make_async_remote_copy(
            src_ref=src,
            dst_ref=cols.at[slot_of(way, dist), kind, part],
            send_sem=z_send.at[way, dist - 1, kind, part],
            recv_sem=z_recv.at[way, dist - 1, kind, part],
            device_id=at_z(1 if way == 0 else -1),
            device_id_type=pl.DeviceIdType.MESH,
        )

    def x_copy(slot, kind, part):
        src = own_part(kind, part) if slot == 0 else cols.at[slot, kind, part]
        return pltpu.make_async_remote_copy(
            src_ref=src,
            dst_ref=cols.at[slot, kind, 3 - part],
            send_sem=x_send.at[slot, kind, part],
            recv_sem=x_recv.at[slot, kind, part],
            device_id=at_x(-1 if part == 0 else 1),
            device_id_type=pl.DeviceIdType.MESH,
        )

    def block_at(to_y):
        return pl.ds(pl.multiple_of(to_y * block_rows, block_rows), block_rows)

    def share_at(dy, dx, of_core):
        owner = (lax.rem(y + dy, ny) * X_HI + lax.rem(x_hi + dx, X_HI)) * CORES + of_core
        return pl.ds(pl.multiple_of(owner * share_rows, share_rows), share_rows)

    def mate_copy(dy, dx):
        return pltpu.make_async_remote_copy(
            src_ref=acc.at[share_at(dy, dx, 1 - core)],
            dst_ref=mate.at[dy, dx],
            send_sem=mate_send.at[dy, dx],
            recv_sem=mate_recv.at[dy, dx],
            device_id=sibling,
            device_id_type=pl.DeviceIdType.MESH,
        )

    def owner_copy(dy, dx):
        return pltpu.make_async_remote_copy(
            src_ref=stage.at[dy, dx],
            dst_ref=landed.at[dy, dx],
            send_sem=red_send.at[dy, dx],
            recv_sem=red_recv.at[dy, dx],
            device_id=at_owner(dy, dx),
            device_id_type=pl.DeviceIdType.MESH,
        )

    subs = [(kind, part) for kind in range(2) for part in range(2)]
    loads = [pltpu.make_async_copy(student, rows, load_sem.at[0])]
    for i, (kind, part) in enumerate(subs):
        loads.append(
            pltpu.make_async_copy(own_part(kind, part), cols.at[0, kind, part], load_sem.at[1 + i])
        )
    for copy in loads:
        copy.start()

    barrier = pltpu.get_barrier_semaphore()
    partners = [at_z(1), at_z(-1), at_x(1), at_x(-1), sibling]
    partners += [at_owner(dy, dx) for dy, dx in owners if (dy, dx) != (0, 0)]
    for partner in partners:
        pl.semaphore_signal(barrier, inc=1, device_id=partner, device_id_type=pl.DeviceIdType.MESH)
    pl.semaphore_wait(barrier, len(partners))

    sent = []

    def send(copy):
        copy.start()
        sent.append(copy)

    for kind, part in subs:
        send(z_copy(0, 1, kind, part))
        send(z_copy(1, 1, kind, part))
        send(x_copy(0, kind, part))

    def pass_on(way, dist, kind, part):
        z_copy(way, dist, kind, part).wait_recv()
        if dist + 1 < half_nz or (dist + 1 == half_nz and part == way):
            send(z_copy(way, dist + 1, kind, part))
        send(x_copy(slot_of(way, dist), kind, part))

    rate = math.log2(math.e) / (WIDEST * width)

    loads[0].wait()

    @pl.loop(0, ny)
    def _(i):
        wide = rows[block_at(i), :].astype(jnp.float32)
        total = jnp.sum(wide * wide, axis=1, keepdims=True)
        norm[block_at(i), :] = jnp.broadcast_to(0.125 - rate * total, (block_rows, 128))

    def columns(slot):
        return cols[slot].reshape(-1, width)

    def column_norm(slot):
        wide = columns(slot).astype(jnp.float32)
        squared = wide * wide
        folded = squared[:, :128]
        for k in range(128, width, 128):
            folded = folded + squared[:, k : k + 128]
        return -rate * jnp.sum(folded.T, axis=0, keepdims=True)

    def weigh(slot, col_norm, where, first):
        col = columns(slot)
        count = col.shape[0]
        inner = lax.dot_general(
            rows[where, :], col, (((1,), (1,)), ((), ())), preferred_element_type=jnp.float32
        )
        row_norm = jnp.concatenate([norm[where, :]] * (count // 128), axis=1)
        f = jnp.exp2(inner * (2.0 * rate) + (row_norm + col_norm))
        f2 = f * f
        f4 = f2 * f2
        f8 = f4 * f4
        summed = f * (LOW + f * (MID + f2 * (HIGH + f4 * (1.0 + f8))))
        near = summed[:, : count // 2]
        far = -summed[:, count // 2 :]
        weights = jnp.concatenate([near, far], axis=1).astype(jnp.bfloat16)
        wide = weights.astype(jnp.float32)
        folded = wide[:, :128]
        for k in range(128, count, 128):
            folded = folded + wide[:, k : k + 128]
        pulled = jnp.dot(weights, col, preferred_element_type=jnp.float32)
        if first:
            mass[where, :] = folded
            acc[where, :] = pulled
        else:
            mass[where, :] += folded
            acc[where, :] += pulled

    def wait_x(slot):
        for kind, part in subs:
            x_copy(slot, kind, part).wait_recv()

    def use(slot, first=False):
        wait_x(slot)
        col_norm = column_norm(slot)

        @pl.loop(0, ny)
        def _(i):
            weigh(slot, col_norm, block_at(i), first)

    def arrive(dist, picked):
        for kind, part in picked:
            for way in range(2):
                if dist < half_nz or part == way:
                    pass_on(way, dist, kind, part)

    arrive(1, subs[:2])
    for copy in loads[1:]:
        copy.wait()
    use(0, first=True)
    arrive(1, subs[2:])
    for dist in range(2, half_nz):
        arrive(dist, subs[:2])
        use(slot_of(0, dist - 1))
        arrive(dist, subs[2:3])
        use(slot_of(1, dist - 1))
        arrive(dist, subs[3:])
    arrive(half_nz, subs)
    use(slot_of(0, half_nz - 1))
    use(slot_of(1, half_nz - 1))

    last = nz - 1
    wait_x(last)
    last_norm = column_norm(last)

    def hand_over(dy):
        for dx in range(X_HI):
            mate_copy(dy, dx).wait_recv()
            total = acc[share_at(dy, dx, core), :] + mate[dy, dx]
            if (dy, dx) == (0, 0):
                out[...] = total
            else:
                stage[dy, dx] = total.astype(jnp.bfloat16)
                send(owner_copy(dy, dx))

    order = list(range(1, ny)) + [0]
    for i, dy in enumerate(order):
        where = block_at(lax.rem(y + dy, ny))
        weigh(last, last_norm, where, False)
        diff = jnp.sum(mass[where, :], axis=1, keepdims=True)
        acc[where, :] -= diff * rows[where, :].astype(jnp.float32)
        for dx in range(X_HI):
            send(mate_copy(dy, dx))
        if i > 0:
            hand_over(order[i - 1])
    hand_over(order[-1])

    total = out[...]
    for dy, dx in owners:
        if (dy, dx) != (0, 0):
            owner_copy(dy, dx).wait_recv()
            total = total + landed[dy, dx].astype(jnp.float32)
    out[...] = total * (1.0 / (groups * local_rows))
    for copy in sent:
        copy.wait_send()


def local(student, teacher):
    groups, blks = lax.axis_size("group"), lax.axis_size("blk")
    local_rows, width = student.shape
    nz, ny = groups // X_LO, blks // (X_HI * CORES)
    share_rows = local_rows // blks
    part_rows = local_rows // (ny * X * CORES)
    dma = pltpu.SemaphoreType.DMA
    pairs = groups * local_rows * 2 * groups * local_rows // (groups * blks)
    return pl.pallas_call(
        functools.partial(kernel, groups=groups, blks=blks),
        out_shape=jax.ShapeDtypeStruct((share_rows, width), jnp.float32),
        in_specs=[pl.BlockSpec(memory_space=pl.ANY)] * 2,
        out_specs=pl.BlockSpec(memory_space=pltpu.VMEM),
        scratch_shapes=[
            pltpu.VMEM((local_rows, width), jnp.bfloat16),
            pltpu.VMEM((nz, 2, 4, part_rows, width), jnp.bfloat16),
            pltpu.VMEM((local_rows, width), jnp.float32),
            pltpu.VMEM((local_rows, 128), jnp.float32),
            pltpu.VMEM((local_rows, 128), jnp.float32),
            pltpu.VMEM((ny, X_HI, share_rows, width), jnp.float32),
            pltpu.VMEM((ny, X_HI, share_rows, width), jnp.bfloat16),
            pltpu.VMEM((ny, X_HI, share_rows, width), jnp.bfloat16),
            dma((5,)),
            dma((2, nz // 2, 2, 2)),
            dma((2, nz // 2, 2, 2)),
            dma((nz, 2, 2)),
            dma((nz, 2, 2)),
            dma((ny, X_HI)),
            dma((ny, X_HI)),
            dma((ny, X_HI)),
            dma((ny, X_HI)),
        ],
        compiler_params=pltpu.CompilerParams(
            collective_id=0, has_side_effects=True, vmem_limit_bytes=48 * 1024 * 1024
        ),
        cost_estimate=pl.CostEstimate(
            flops=4 * pairs * width, bytes_accessed=8 * 1024 * 1024, transcendentals=pairs
        ),
    )(student, teacher)


def solution(mesh):
    in_specs = (P("group", None), P("group", None))
    out_specs = P(("group", "blk"), None)
    return jax.shard_map(local, mesh=mesh, in_specs=in_specs, out_specs=out_specs, check_vma=False)
```

time: 355 us -> 76.1 us (0.21)
  the two profiles are of different devices: /device:TPU:8 before, /device:TPU:1 now
where the time goes in v1:
time: 76.1 us; the launch traced here: 75.9 us
  Pallas kernels  72 us (95%)
  local copies, waits for them, and re-layouts  3.89 us (5%)
    pallas_call x1, Pallas kernels, local(): pl.pallas_call(functools.partial(kernel, groups=groups, blks=blks), out_s...  72 us
    unnamed x5, local copies, waits for them, and re-layouts  3.89 us

profile of v1, /device:TPU:1, one launch (start us, length us, event | category | flops | bytes accessed | tf_op | source)
XLA Modules:
  0.0 75.9 jit_solution(1140814289751984234)
XLA Ops:
  0.0 0.0 copy-start
  0.0 1.6 %copy-done = bf16[1024,1024]{1,0:T(8,128)(2,1)S(1)} copy-done((bf16[1024,1024]{1,0:T(8,128)(2,1)S(1)}, bf16[1024,1024]{1,0:T(8,128)(2,1)}, u32[]{:S(2)}) %copy-start) | copy-done | bytes 2097176
  1.6 0.0 copy-start.1
  1.6 1.6 %copy-done.1 = bf16[1024,1024]{1,0:T(8,128)(2,1)S(1)} copy-done((bf16[1024,1024]{1,0:T(8,128)(2,1)S(1)}, bf16[1024,1024]{1,0:T(8,128)(2,1)}, u32[]{:S(2)}) %copy-start.1) | copy-done | bytes 2097176
  3.2 72.0 %shard_map.28 = f32[64,1024]{1,0:T(8,128)S(1)} custom-call(bf16[1024,1024]{1,0:T(8,128)(2,1)S(1)} %copy-done, bf16[1024,1024]{1,0:T(8,128)(2,1)S(1)} %copy-done.1), custom_call_target="tpu_custom_call" | custom-call | flops 8589934592 | bytes 8388608 | tf_op jit(solution)/shard_map/pallas_call | solution.py:276
  75.2 0.7 copy.4
Async XLA Ops:
  0.0 1.6 %copy-start = (bf16[1024,1024]{1,0:T(8,128)(2,1)S(1)}, bf16[1024,1024]{1,0:T(8,128)(2,1)}, u32[]{:S(2)}) copy-start(bf16[1024,1024]{1,0:T(8,128)(2,1)} %student.1) | copy-start | bytes 6291460
  1.6 1.6 %copy-start.1 = (bf16[1024,1024]{1,0:T(8,128)(2,1)S(1)}, bf16[1024,1024]{1,0:T(8,128)(2,1)}, u32[]{:S(2)}) copy-start(bf16[1024,1024]{1,0:T(8,128)(2,1)} %teacher.1) | copy-start | bytes 6291460

commit v2 on v1

--- a/solution.py
+++ b/solution.py
@@ -64,7 +64,7 @@
             return 0
         if dist == half_nz:
             return nz - 1
-        return dist if way == 0 else half_nz - 1 + dist
+        return 2 * dist - 1 + way
 
     def z_copy(way, dist, kind, part):
         src = own_part(kind, part) if dist == 1 else cols.at[slot_of(way, dist - 1), kind, part]
@@ -137,10 +137,13 @@
         copy.start()
         sent.append(copy)
 
-    for kind, part in subs:
-        send(z_copy(0, 1, kind, part))
-        send(z_copy(1, 1, kind, part))
-        send(x_copy(0, kind, part))
+    def sub_of(way, i):
+        return i // 2, (i + way) % 2
+
+    for i in range(4):
+        for way in range(2):
+            send(z_copy(way, 1, *sub_of(way, i)))
+        send(x_copy(0, *subs[i]))
 
     def pass_on(way, dist, kind, part):
         z_copy(way, dist, kind, part).wait_recv()
@@ -158,37 +161,40 @@
         total = jnp.sum(wide * wide, axis=1, keepdims=True)
         norm[block_at(i), :] = jnp.broadcast_to(0.125 - rate * total, (block_rows, 128))
 
-    def columns(slot):
-        return cols[slot].reshape(-1, width)
-
-    def column_norm(slot):
-        wide = columns(slot).astype(jnp.float32)
+    def columns(slot, count):
+        return cols[slot : slot + count].reshape(-1, width)
+
+    def column_norm(slot, count):
+        wide = columns(slot, count).astype(jnp.float32)
         squared = wide * wide
         folded = squared[:, :128]
         for k in range(128, width, 128):
             folded = folded + squared[:, k : k + 128]
         return -rate * jnp.sum(folded.T, axis=0, keepdims=True)
 
-    def weigh(slot, col_norm, where, first):
-        col = columns(slot)
-        count = col.shape[0]
+    def weigh(slot, count, col_norm, where, first=False):
+        col = columns(slot, count)
         inner = lax.dot_general(
             rows[where, :], col, (((1,), (1,)), ((), ())), preferred_element_type=jnp.float32
         )
-        row_norm = jnp.concatenate([norm[where, :]] * (count // 128), axis=1)
-        f = jnp.exp2(inner * (2.0 * rate) + (row_norm + col_norm))
-        f2 = f * f
-        f4 = f2 * f2
-        f8 = f4 * f4
-        summed = f * (LOW + f * (MID + f2 * (HIGH + f4 * (1.0 + f8))))
-        near = summed[:, : count // 2]
-        far = -summed[:, count // 2 :]
-        weights = jnp.concatenate([near, far], axis=1).astype(jnp.bfloat16)
-        wide = weights.astype(jnp.float32)
-        folded = wide[:, :128]
-        for k in range(128, count, 128):
-            folded = folded + wide[:, k : k + 128]
-        pulled = jnp.dot(weights, col, preferred_element_type=jnp.float32)
+        lanes = 4 * part_rows
+        row_norm = norm[where, :]
+        weights = []
+        folded = None
+        for k in range(2 * count):
+            span = slice(k * lanes, (k + 1) * lanes)
+            f = jnp.exp2(inner[:, span] * (2.0 * rate) + (row_norm + col_norm[:, span]))
+            f2 = f * f
+            f4 = f2 * f2
+            f8 = f4 * f4
+            summed = f * (LOW + f * (MID + f2 * (HIGH + f4 * (1.0 + f8))))
+            weight = (summed if k % 2 == 0 else -summed).astype(jnp.bfloat16)
+            weights.append(weight)
+            wide = weight.astype(jnp.float32)
+            folded = wide if folded is None else folded + wide
+        pulled = jnp.dot(
+            jnp.concatenate(weights, axis=1), col, preferred_element_type=jnp.float32
+        )
         if first:
             mass[where, :] = folded
             acc[where, :] = pulled
@@ -200,38 +206,48 @@
         for kind, part in subs:
             x_copy(slot, kind, part).wait_recv()
 
-    def use(slot, first=False):
-        wait_x(slot)
-        col_norm = column_norm(slot)
-
-        @pl.loop(0, ny)
-        def _(i):
-            weigh(slot, col_norm, block_at(i), first)
-
-    def arrive(dist, picked):
-        for kind, part in picked:
-            for way in range(2):
-                if dist < half_nz or part == way:
-                    pass_on(way, dist, kind, part)
-
-    arrive(1, subs[:2])
+    def half_rows(i):
+        return slice(i * local_rows // 2, (i + 1) * local_rows // 2)
+
+    def arrive(dist, i):
+        for way in range(2):
+            pass_on(way, dist, *sub_of(way, i))
+
     for copy in loads[1:]:
         copy.wait()
-    use(0, first=True)
-    arrive(1, subs[2:])
+    arrive(1, 0)
+    arrive(1, 1)
+    wait_x(0)
+    col_norm = column_norm(0, 1)
+    for i in range(2):
+        weigh(0, 1, col_norm, half_rows(i), first=True)
+    arrive(1, 2)
+    arrive(1, 3)
     for dist in range(2, half_nz):
-        arrive(dist, subs[:2])
-        use(slot_of(0, dist - 1))
-        arrive(dist, subs[2:3])
-        use(slot_of(1, dist - 1))
-        arrive(dist, subs[3:])
-    arrive(half_nz, subs)
-    use(slot_of(0, half_nz - 1))
-    use(slot_of(1, half_nz - 1))
+        slot = slot_of(0, dist - 1)
+        arrive(dist, 0)
+        arrive(dist, 1)
+        wait_x(slot)
+        wait_x(slot + 1)
+        col_norm = column_norm(slot, 2)
+        weigh(slot, 2, col_norm, half_rows(0))
+        arrive(dist, 2)
+        weigh(slot, 2, col_norm, half_rows(1))
+        arrive(dist, 3)
+    for i in (0, 2):
+        arrive(half_nz, i)
+    slot = slot_of(0, half_nz - 1)
+    wait_x(slot)
+    wait_x(slot + 1)
+    col_norm = column_norm(slot, 2)
+    for i in range(2):
+        weigh(slot, 2, col_norm, half_rows(i))
 
     last = nz - 1
     wait_x(last)
-    last_norm = column_norm(last)
+    last_norm = column_norm(last, 1)
+    gathered = sent
+    sent = []
 
     def hand_over(dy):
         for dx in range(X_HI):
@@ -243,10 +259,10 @@
                 stage[dy, dx] = total.astype(jnp.bfloat16)
                 send(owner_copy(dy, dx))
 
-    order = list(range(1, ny)) + [0]
+    order = [2, 1, 3, 0] if ny == 4 else list(range(ny))
     for i, dy in enumerate(order):
         where = block_at(lax.rem(y + dy, ny))
-        weigh(last, last_norm, where, False)
+        weigh(last, 1, last_norm, where)
         diff = jnp.sum(mass[where, :], axis=1, keepdims=True)
         acc[where, :] -= diff * rows[where, :].astype(jnp.float32)
         for dx in range(X_HI):
@@ -255,6 +271,8 @@
             hand_over(order[i - 1])
     hand_over(order[-1])
 
+    for copy in gathered:
+        copy.wait_send()
     total = out[...]
     for dy, dx in owners:
         if (dy, dx) != (0, 0):
@@ -298,7 +316,7 @@
             dma((ny, X_HI)),
         ],
         compiler_params=pltpu.CompilerParams(
-            collective_id=0, has_side_effects=True, vmem_limit_bytes=48 * 1024 * 1024
+            collective_id=0, has_side_effects=True, vmem_limit_bytes=60 * 1024 * 1024
         ),
         cost_estimate=pl.CostEstimate(
             flops=4 * pairs * width, bytes_accessed=8 * 1024 * 1024, transcendentals=pairs

time: 76.1 us -> 65.3 us (0.86)
  Pallas kernels: 72 us -> 63.5 us
  local copies, waits for them, and re-layouts: 3.89 us -> 1.67 us
    pallas_call x1, Pallas kernels: 72 us -> 63.5 us  [local(): pl.pallas_call(functools.partial(kernel, groups=groups, blks=blks), out_s...]
    unnamed x5 -> x1, local copies, waits for them, and re-layouts: 3.89 us -> 1.67 us
where the time goes in v2:
time: 65.3 us; the launch traced here: 65.2 us
  Pallas kernels  63.5 us (97%)
  local copies, waits for them, and re-layouts  1.67 us (3%)
    pallas_call x1, Pallas kernels, local(): pl.pallas_call(functools.partial(kernel, groups=groups, blks=blks), out_s...  63.5 us
    unnamed x1, local copies, waits for them, and re-layouts  1.67 us

profile of v2, /device:TPU:1, one launch (start us, length us, event | category | flops | bytes accessed | tf_op | source)
XLA Modules:
  0.0 65.2 jit_solution(8092296215823735777)
XLA Ops:
  0.0 63.5 %shard_map.28 = f32[64,1024]{1,0:T(8,128)} custom-call(bf16[1024,1024]{1,0:T(8,128)(2,1)} %student.1, bf16[1024,1024]{1,0:T(8,128)(2,1)} %teacher.1), custom_call_target="tpu_custom_call" | custom-call | flops 8589934592 | bytes 8388608 | tf_op jit(solution)/shard_map/pallas_call | solution.py:294
  63.5 1.7 %copy.4 = f32[64,1024]{1,0:T(8,128)} copy(f32[64,1024]{1,0:T(8,128)} %shard_map.28) | data formatting | bytes 524288

commit v3 on v0

v3 whole, which is shorter than its diff:
```python
import functools
import math

import jax
import jax.numpy as jnp
from jax import lax
from jax.experimental import pallas as pl
from jax.experimental.pallas import tpu as pltpu
from jax.sharding import PartitionSpec as P

X_HI = 2
X_LO = 2
CORES = 2
X = X_HI * X_LO
WIDEST = 8.0

LOW = 0.25 * 2.0 ** -0.125
MID = 0.5 * 2.0 ** -0.25
HIGH = 2.0 ** -0.5


def kernel(student, teacher, out, rows, cols, acc, norm, mass, stage, landed,
           row_sem, load_sem, first_send, first_recv, split_send, z_send, z_recv, x_send, x_recv, mate_send, mate_recv,
           red_send, red_recv, *, groups, blks):
    nz = groups // X_LO
    ny = blks // (X_HI * CORES)
    width = rows.shape[1]
    part_rows = cols.shape[5]
    share_rows = rows.shape[0] // (ny * X_HI)
    half_nz = nz // 2
    last = nz - 1

    group = lax.axis_index("group")
    blk = lax.axis_index("blk")
    x_lo, z = group // nz, lax.rem(group, nz)
    y, x_hi, core = blk // (X_HI * CORES), lax.rem(blk // CORES, X_HI), lax.rem(blk, CORES)
    x = x_hi * X_LO + x_lo

    def at_z(step):
        return {"group": x_lo * nz + lax.rem(z + step + nz, nz), "blk": blk}

    def at_x(step):
        to = lax.rem(x + step + X, X)
        return {
            "group": lax.rem(to, X_LO) * nz + z,
            "blk": (y * X_HI + to // X_LO) * CORES + core,
        }

    def share_of(dy, dx):
        return (lax.rem(y + dy, ny) * X_HI + lax.rem(x_hi + dx, X_HI)) * CORES + core

    def at_owner(dy, dx):
        return {"group": group, "blk": share_of(dy, dx)}

    sibling = {"group": group, "blk": blk + 1 - 2 * core}
    owners = [(dy, dx) for dy in ([2, 1, 3, 0] if ny == 4 else range(ny - 1, -1, -1)) for dx in (1, 0)]
    sources = (student, teacher)

    def remote(src, dst, send_sem, recv_sem, to):
        return pltpu.make_async_remote_copy(
            src_ref=src,
            dst_ref=dst,
            send_sem=send_sem,
            recv_sem=recv_sem,
            device_id=to,
            device_id_type=pl.DeviceIdType.MESH,
        )

    def own_part(kind, part, of_core):
        quarter = lax.rem(x + part, X)
        start = ((y * X + quarter) * CORES + of_core) * part_rows
        return sources[kind].at[pl.ds(pl.multiple_of(start, part_rows), part_rows)]

    def slot_of(way, dist):
        if dist == 0:
            return 0
        if dist == half_nz:
            return last
        return 2 * dist - 1 + way

    def z_copy(way, dist, part):
        at = (way, dist - 1, part)
        return remote(
            cols.at[slot_of(way, dist - 1), 0, 0, part],
            cols.at[slot_of(way, dist), 0, 0, part],
            z_send.at[at],
            z_recv.at[at],
            at_z(1 if way == 0 else -1),
        )

    def z_first(way, part, kind):
        at = (way, part, kind)
        return remote(
            own_part(kind, part, core),
            cols.at[slot_of(way, 1), 0, 0, part, kind],
            first_send.at[at],
            first_recv.at[at],
            at_z(1 if way == 0 else -1),
        )

    def x_copy(slot, part, kind=None):
        src, dst = cols.at[slot, 0, 0, part], cols.at[slot, 1, 0, 1 - part]
        send_sem = x_send.at[slot, part]
        if kind is not None:
            src = own_part(kind, part, core) if slot == 0 else src.at[kind]
            dst, send_sem = dst.at[kind], split_send.at[slot, part, kind]
        return remote(src, dst, send_sem, x_recv.at[slot, part], at_x(-1 if part == 0 else 1))

    def mate_copy(slot, half, part):
        at = (slot, half, part)
        return remote(
            cols.at[slot, half, 0, part],
            cols.at[slot, half, 1, part],
            mate_send.at[at],
            mate_recv.at[at],
            sibling,
        )

    def owner_copy(i):
        return remote(stage.at[i], landed.at[i], red_send.at[i], red_recv.at[i], at_owner(*owners[i]))

    subs = [(kind, part) for kind in range(2) for part in range(2)]

    barrier = pltpu.get_barrier_semaphore()
    partners = [at_z(1), at_z(-1), at_x(1), at_x(-1), sibling]
    partners += [at_owner(dy, dx) for dy, dx in owners if (dy, dx) != (0, 0)]
    for partner in partners:
        pl.semaphore_signal(barrier, inc=1, device_id=partner, device_id_type=pl.DeviceIdType.MESH)

    row_loads = []
    for i, (dy, dx) in enumerate(owners):
        start = pl.multiple_of(share_of(dy, dx) * share_rows, share_rows)
        row_loads.append(
            pltpu.make_async_copy(
                student.at[pl.ds(start, share_rows)],
                rows.at[pl.ds(i * share_rows, share_rows)],
                row_sem.at[i],
            )
        )
    col_loads = []
    for who in range(2):
        of_core = core if who == 0 else 1 - core
        for kind, part in subs:
            col_loads.append(
                pltpu.make_async_copy(
                    own_part(kind, part, of_core),
                    cols.at[0, 0, who, part, kind],
                    load_sem.at[who, kind, part],
                )
            )
    for copy in row_loads + col_loads:
        copy.start()
    pl.semaphore_wait(barrier, len(partners))

    gathered = []

    def send(copy, sent=gathered):
        copy.start()
        sent.append(copy)

    for i in range(2):
        for kind in range(2):
            for way in range(2):
                send(z_first(way, (i + way) % 2, kind))
            send(x_copy(0, i, kind))

    rate = math.log2(math.e) / (WIDEST * width)
    lanes = 4 * part_rows
    lane = lax.broadcasted_iota(jnp.int32, (1, lanes), 1)
    sign = jnp.where(lax.rem(lane, 2 * part_rows) < part_rows, 1.0, -1.0)

    for copy in row_loads:
        copy.wait()
    for copy in col_loads:
        copy.wait()
    wide_rows = rows[...].astype(jnp.float32)
    row_squares = jnp.sum(wide_rows * wide_rows, axis=1, keepdims=True)
    norm[...] = jnp.broadcast_to(0.125 - rate * row_squares, norm.shape)

    def weigh(read, where):
        col = read().reshape(-1, width)
        wide_col = col.astype(jnp.float32)
        squared = wide_col * wide_col
        folded = squared[:, :128]
        for k in range(128, width, 128):
            folded = folded + squared[:, k : k + 128]
        col_norm = -rate * jnp.sum(folded.T, axis=0, keepdims=True)
        inner = lax.dot_general(
            rows[where, :], col, (((1,), (1,)), ((), ())), preferred_element_type=jnp.float32
        )
        row_norm = norm[where, :]
        weights = []
        folded = None
        for k in range(0, col.shape[0], lanes):
            f = jnp.exp2(
                inner[:, k : k + lanes] * (2.0 * rate) + (row_norm + col_norm[:, k : k + lanes])
            )
            f2 = f * f
            f4 = f2 * f2
            f8 = f4 * f4
            summed = f * (LOW + f * (MID + f2 * (HIGH + f4 * (1.0 + f8))))
            weight = (summed * sign).astype(jnp.bfloat16)
            weights.append(weight)
            wide = weight.astype(jnp.float32)
            folded = wide if folded is None else folded + wide
        pulled = jnp.dot(
            jnp.concatenate(weights, axis=1), col, preferred_element_type=jnp.float32
        )
        return folded, pulled

    def use(read, first=False):
        folded, pulled = weigh(read, slice(0, rows.shape[0]))
        if first:
            mass[...] = folded
            acc[...] = pulled
        else:
            mass[...] += folded
            acc[...] += pulled

    def events(dist, i):
        ways = range(2)
        return [(slot_of(way, dist), way, (i + way) % 2) for way in ways]

    def arrive(dist, i):
        if dist == 1:
            for kind in range(2):
                for slot, way, part in events(dist, i):
                    z_first(way, part, kind).wait_recv()
                    send(x_copy(slot, part, kind))
        for slot, way, part in events(dist, i):
            if dist > 1:
                z_copy(way, dist, part).wait_recv()
                send(x_copy(slot, part))
            if dist + 1 < half_nz or (dist + 1 == half_nz and part == way):
                send(z_copy(way, dist + 1, part))
            send(mate_copy(slot, 0, part))

    def cross(dist, i):
        for slot, way, part in events(dist, i):
            x_copy(slot, part).wait_recv()
            send(mate_copy(slot, 1, 1 - part))

    def take(slots, half):
        for slot in slots:
            for part in range(2):
                mate_copy(slot, half, part).wait_recv()

    def use_pair(dist, half):
        slot = slot_of(0, dist)
        take((slot, slot + 1), half)
        use(lambda: cols[slot : slot + 2, half])

    arrive(1, 0)
    for part in range(2):
        x_copy(0, part).wait_recv()
        send(mate_copy(0, 1, 1 - part))
    arrive(1, 1)
    take((0,), 1)
    use(lambda: cols[0], first=True)
    cross(1, 0)
    for dist in range(2, half_nz):
        arrive(dist, 0)
        use_pair(dist - 1, 0)
        cross(dist - 1, 1)
        arrive(dist, 1)
        use_pair(dist - 1, 1)
        cross(dist, 0)
    arrive(half_nz, 0)
    use_pair(half_nz - 1, 0)
    cross(half_nz - 1, 1)
    take((last,), 0)
    use(lambda: cols[last, 0])
    cross(half_nz, 0)
    use_pair(half_nz - 1, 1)
    take((last,), 1)

    reduced = []
    batch = min(4, len(owners))
    for begin in range(0, len(owners), batch):
        where = slice(begin * share_rows, (begin + batch) * share_rows)
        folded, pulled = weigh(lambda: cols[last, 1], where)
        diff = jnp.sum(mass[where, :] + folded, axis=1, keepdims=True)
        total = acc[where, :] + pulled - diff * rows[where, :].astype(jnp.float32)
        for i in range(begin, begin + batch):
            share = total[(i - begin) * share_rows : (i - begin + 1) * share_rows]
            if owners[i] == (0, 0):
                acc[i * share_rows : (i + 1) * share_rows, :] = share
            else:
                stage[i] = share.astype(jnp.bfloat16)
                send(owner_copy(i), reduced)

    for copy in gathered:
        copy.wait_send()
    total = acc[(len(owners) - 1) * share_rows :, :]
    for i in range(len(owners) - 1):
        owner_copy(i).wait_recv()
        total = total + landed[i].astype(jnp.float32)
    out[...] = total * (1.0 / (groups * blks * share_rows))
    for copy in reduced:
        copy.wait_send()


def local(student, teacher):
    groups, blks = lax.axis_size("group"), lax.axis_size("blk")
    local_rows, width = student.shape
    nz, ny = groups // X_LO, blks // (X_HI * CORES)
    share_rows = local_rows // blks
    part_rows = local_rows // (ny * X * CORES)
    core_rows = local_rows // CORES
    dma = pltpu.SemaphoreType.DMA
    pairs = groups * local_rows * 2 * groups * local_rows // (groups * blks)
    return pl.pallas_call(
        functools.partial(kernel, groups=groups, blks=blks),
        out_shape=jax.ShapeDtypeStruct((share_rows, width), jnp.float32),
        in_specs=[pl.BlockSpec(memory_space=pltpu.HBM)] * 2,
        out_specs=pl.BlockSpec(memory_space=pltpu.VMEM),
        scratch_shapes=[
            pltpu.VMEM((core_rows, width), jnp.bfloat16),
            pltpu.VMEM((nz, 2, CORES, 2, 2, part_rows, width), jnp.bfloat16),
            pltpu.VMEM((core_rows, width), jnp.float32),
            pltpu.VMEM((core_rows, 128), jnp.float32),
            pltpu.VMEM((core_rows, 128), jnp.float32),
            pltpu.VMEM((ny * X_HI, share_rows, width), jnp.bfloat16),
            pltpu.VMEM((ny * X_HI, share_rows, width), jnp.bfloat16),
            dma((ny * X_HI,)),
            dma((CORES, 2, 2)),
            dma((2, 2, 2)),
            dma((2, 2, 2)),
            dma((3, 2, 2)),
            dma((2, nz // 2, 2)),
            dma((2, nz // 2, 2)),
            dma((nz, 2)),
            dma((nz, 2)),
            dma((nz, 2, 2)),
            dma((nz, 2, 2)),
            dma((ny * X_HI,)),
            dma((ny * X_HI,)),
        ],
        compiler_params=pltpu.CompilerParams(
            collective_id=0, has_side_effects=True, vmem_limit_bytes=52 * 1024 * 1024
        ),
        cost_estimate=pl.CostEstimate(
            flops=4 * pairs * width, bytes_accessed=8 * 1024 * 1024, transcendentals=pairs
        ),
    )(student, teacher)


def solution(mesh):
    in_specs = (P("group", None), P("group", None))
    out_specs = P(("group", "blk"), None)
    return jax.shard_map(local, mesh=mesh, in_specs=in_specs, out_specs=out_specs, check_vma=False)
```

time: 355 us -> 56.7 us (0.16)
  the two profiles are of different devices: /device:TPU:8 before, /device:TPU:1 now
where the time goes in v3:
time: 56.7 us; the launch traced here: 56.6 us
  Pallas kernels  55.9 us (99%)
  local copies, waits for them, and re-layouts  0.71 us (1%)
    pallas_call x1, Pallas kernels, local(): pl.pallas_call(functools.partial(kernel, groups=groups, blks=blks), out_s...  55.9 us

profile of v3, /device:TPU:1, one launch (start us, length us, event | category | flops | bytes accessed | tf_op | source)
XLA Modules:
  0.0 56.6 jit_solution(8747254247978125484)
XLA Ops:
  0.0 55.9 %shard_map.28 = f32[64,1024]{1,0:T(8,128)S(1)} custom-call(bf16[1024,1024]{1,0:T(8,128)(2,1)} %student.1, bf16[1024,1024]{1,0:T(8,128)(2,1)} %teacher.1), custom_call_target="tpu_custom_call" | custom-call | flops 8589934592 | bytes 8388608 | tf_op jit(solution)/shard_map/pallas_call | solution.py:312
  55.9 0.7 %copy.4 = f32[64,1024]{1,0:T(8,128)} copy(f32[64,1024]{1,0:T(8,128)S(1)} %shard_map.28) | data formatting | bytes 524288

commit v4 on v0

v4 whole, which is shorter than its diff:
```python
import functools
import math

import jax
import jax.numpy as jnp
from jax import lax
from jax.experimental import pallas as pl
from jax.experimental.pallas import tpu as pltpu
from jax.sharding import PartitionSpec as P

X_HI = 2
X_LO = 2
CORES = 2
X = X_HI * X_LO
WIDEST = 8.0

LOW = 0.25 * 2.0 ** -0.125
MID = 0.5 * 2.0 ** -0.25
HIGH = 2.0 ** -0.5


SCALE = 2.0**9


def encode(value):
    scaled = value * SCALE
    squared = scaled * scaled
    return (squared * scaled * jnp.abs(scaled)).astype(jnp.bfloat16)


def decode(code):
    wide = code.astype(jnp.float32)
    root = lax.rsqrt(lax.rsqrt(jnp.abs(wide))) * (1.0 / SCALE)
    return jnp.where(wide < 0.0, -root, root)


def kernel(student, teacher, out, cols, col_norm, rows, norm, mass, res, x_out, x_in, z_out, z_in, far_out, far_in,
           load_sem, own_sem, z_send, z_recv, x_send, x_recv,
           x_back_send, x_back_recv, z_back_send, z_back_recv, far_send, far_recv, *, groups, blks):
    nz = groups // X_LO
    width = cols.shape[1]
    part_rows = rows.shape[3]
    share_rows = 2 * part_rows
    local_rows = cols.shape[0] // 2
    half_nz = nz // 2
    last = nz - 1

    group = lax.axis_index("group")
    blk = lax.axis_index("blk")
    x_lo, z = group // nz, lax.rem(group, nz)
    y, x_hi, core = blk // (X_HI * CORES), lax.rem(blk // CORES, X_HI), lax.rem(blk, CORES)
    x = x_hi * X_LO + x_lo

    def at_z(step):
        return {"group": x_lo * nz + lax.rem(z + step + nz, nz), "blk": blk}

    def at_x(step):
        to = lax.rem(x + step + X, X)
        return {
            "group": lax.rem(to, X_LO) * nz + z,
            "blk": (y * X_HI + to // X_LO) * CORES + core,
        }

    def remote(src, dst, send_sem, recv_sem, to):
        return pltpu.make_async_remote_copy(
            src_ref=src,
            dst_ref=dst,
            send_sem=send_sem,
            recv_sem=recv_sem,
            device_id=to,
            device_id_type=pl.DeviceIdType.MESH,
        )

    def away(way):
        return 1 if way == 0 else -1

    def own_part(part):
        start = blk * share_rows + part * part_rows
        return student.at[pl.ds(pl.multiple_of(start, part_rows), part_rows)]

    def slot_of(way, dist):
        if dist == 0:
            return 0
        if dist == half_nz:
            return last
        return 2 * dist - 1 + way

    def z_copy(way, dist, part):
        at = (way, dist - 1, part)
        src = own_part(part) if dist == 1 else rows.at[slot_of(way, dist - 1), 0, part]
        return remote(
            src, rows.at[slot_of(way, dist), 0, part], z_send.at[at], z_recv.at[at], at_z(away(way))
        )

    def x_copy(slot, part):
        src = own_part(part) if slot == 0 else rows.at[slot, 0, part]
        at = (slot, part)
        return remote(
            src, rows.at[slot, 1, 1 - part], x_send.at[at], x_recv.at[at], at_x(-1 if part == 0 else 1)
        )

    def x_back(slot, index):
        at = (slot, index)
        return remote(
            x_out.at[at],
            x_in.at[slot, 1 - index],
            x_back_send.at[at],
            x_back_recv.at[slot, 1 - index],
            at_x(1 if index == 1 else -1),
        )

    def wait_x_back(slot, part):
        at = (slot, part)
        remote(
            x_out.at[at], x_in.at[at], x_back_send.at[at], x_back_recv.at[at], at_x(1)
        ).wait_recv()

    def z_back(way, dist, part):
        at = (way, dist - 1, part)
        return remote(
            z_out.at[at], z_in.at[at], z_back_send.at[at], z_back_recv.at[at], at_z(-away(way))
        )

    def far_back(part):
        return remote(
            far_out.at[part], far_in.at[part], far_send.at[part], far_recv.at[part], at_z(half_nz)
        )

    loads = [
        pltpu.make_async_copy(student, cols.at[pl.ds(0, local_rows)], load_sem.at[0]),
        pltpu.make_async_copy(teacher, cols.at[pl.ds(local_rows, local_rows)], load_sem.at[1]),
    ]
    loads += [
        pltpu.make_async_copy(own_part(part), rows.at[0, 0, part], own_sem.at[part])
        for part in range(2)
    ]
    barrier = pltpu.get_barrier_semaphore()
    partners = [at_z(1), at_z(-1), at_x(1), at_x(-1), at_z(half_nz)]
    for partner in partners:
        pl.semaphore_signal(barrier, inc=1, device_id=partner, device_id_type=pl.DeviceIdType.MESH)
    for copy in loads:
        copy.start()
    pl.semaphore_wait(barrier, len(partners))

    sent = []

    def send(copy):
        copy.start()
        sent.append(copy)

    for i in range(2):
        for way in range(2):
            send(z_copy(way, 1, (i + way) % 2))
        send(x_copy(0, i))

    rate = math.log2(math.e) / (WIDEST * width)
    for copy in loads:
        copy.wait()

    @pl.loop(0, 2 * local_rows // 256)
    def _(i):
        wide = cols[pl.ds(pl.multiple_of(i * 256, 256), 256), :].astype(jnp.float32)
        squared = wide * wide
        folded = squared[:, :128]
        for k in range(128, width, 128):
            folded = folded + squared[:, k : k + 128]
        col_norm[i, :, :] = jnp.broadcast_to(-rate * jnp.sum(folded.T, axis=0, keepdims=True), (8, 256))

    step = 512

    def weigh(row, row_norm, begin):
        col = cols[begin : begin + step, :]
        inner = lax.dot_general(
            row, col, (((1,), (1,)), ((), ())), preferred_element_type=jnp.float32
        )
        weights = []
        folded = None
        for k in range(0, step, 128):
            at = (begin + k) // 256
            norms = col_norm[at, 0:1, :][:, (begin + k) % 256 : (begin + k) % 256 + 128]
            f = jnp.exp2(inner[:, k : k + 128] * (2.0 * rate) + (row_norm + norms))
            f2 = f * f
            f4 = f2 * f2
            f8 = f4 * f4
            summed = f * (LOW + f * (MID + f2 * (HIGH + f4 * (1.0 + f8))))
            weight = (summed if begin < local_rows else -summed).astype(jnp.bfloat16)
            weights.append(weight)
            wide = weight.astype(jnp.float32)
            folded = wide if folded is None else folded + wide
        pulled = jnp.dot(
            jnp.concatenate(weights, axis=1), col, preferred_element_type=jnp.float32
        )
        return folded, pulled

    def use(slot, count, quarters=range(4)):
        row = rows[slot : slot + count].reshape(-1, width)
        where = slice(slot * 2 * share_rows, (slot + count) * 2 * share_rows)
        if 0 in quarters:
            wide = row.astype(jnp.float32)
            total = jnp.sum(wide * wide, axis=1, keepdims=True)
            norm[where, :] = jnp.broadcast_to(0.125 - rate * total, (row.shape[0], 128))
        for quarter in quarters:
            folded, pulled = weigh(row, norm[where, :], quarter * step)
            if quarter == 0:
                mass[where, :] = folded
                res[where, :] = pulled
            else:
                mass[where, :] += folded
                res[where, :] += pulled
        if 3 in quarters:
            diff = jnp.sum(mass[where, :], axis=1, keepdims=True)
            whole = res[where, :] - diff * row.astype(jnp.float32)
            res[where, :] = whole
            for c in range(count):
                for index in range(2):
                    start = (2 * c + 1) * share_rows + index * part_rows
                    x_out[slot + c, index] = encode(whole[start : start + part_rows])

    def own_sum(slot, part):
        wait_x_back(slot, part)
        start = slot * 2 * share_rows + part * part_rows
        return res[start : start + part_rows, :] + decode(x_in[slot, part])

    def keep(slot, part):
        start = slot * 2 * share_rows + part * part_rows
        res[start : start + part_rows, :] = own_sum(slot, part)

    def kept(slot, part):
        start = slot * 2 * share_rows + part * part_rows
        return res[start : start + part_rows, :]

    def arrive(dist, i):
        for way in range(2):
            part = (i + way) % 2
            z_copy(way, dist, part).wait_recv()
            if dist + 1 < half_nz or (dist + 1 == half_nz and part == way):
                send(z_copy(way, dist + 1, part))
            send(x_copy(slot_of(way, dist), part))

    def cross(*slots):
        for slot in slots:
            for part in range(2):
                x_copy(slot, part).wait_recv()

    def give_back(*slots):
        for slot in slots:
            for index in range(2):
                send(x_back(slot, index))

    arrive(1, 0)
    arrive(1, 1)
    cross(0)
    use(0, 1)
    for dist in range(2, half_nz):
        slot = slot_of(0, dist - 1)
        if dist == 2:
            arrive(2, 0)
            arrive(2, 1)
        cross(slot, slot + 1)
        use(slot, 2, range(2))
        if dist + 1 < half_nz:
            arrive(dist + 1, 0)
        else:
            arrive(half_nz, 0)
            give_back(0)
            for early in range(1, half_nz - 2):
                give_back(slot_of(0, early), slot_of(1, early))
        use(slot, 2, range(2, 4))
        if dist + 1 < half_nz:
            arrive(dist + 1, 1)
    slot = slot_of(0, half_nz - 2)
    give_back(slot, slot + 1)
    slot = slot_of(0, half_nz - 1)
    cross(slot, slot + 1)
    use(slot, 2)
    give_back(slot, slot + 1)
    cross(last)
    use(last, 1)
    give_back(last)

    for dist in range(half_nz - 1):
        for slot in sorted({slot_of(0, dist), slot_of(1, dist)}):
            for part in range(2):
                keep(slot, part)
    for part in range(2):
        for way in range(2):
            z_out[way, half_nz - 2, part] = encode(own_sum(slot_of(way, half_nz - 1), part))
            send(z_back(way, half_nz - 1, part))
    for part in range(2):
        far_out[part] = encode(own_sum(last, part))
        send(far_back(part))
    for dist in range(half_nz - 2, 0, -1):
        for part in range(2):
            for way in range(2):
                z_back(way, dist + 1, part).wait_recv()
                z_out[way, dist - 1, part] = encode(
                    kept(slot_of(way, dist), part) + decode(z_in[way, dist, part])
                )
                send(z_back(way, dist, part))
    for part in range(2):
        far_back(part).wait_recv()
        res[part * part_rows : (part + 1) * part_rows, :] = kept(0, part) + decode(far_in[part])
    for copy in sent:
        copy.wait_send()
    for part in range(2):
        total = kept(0, part)
        for way in range(2):
            z_back(way, 1, part).wait_recv()
            total = total + decode(z_in[way, 0, part])
        out[part * part_rows : (part + 1) * part_rows, :] = total * (1.0 / (groups * local_rows))


def local(student, teacher):
    groups, blks = lax.axis_size("group"), lax.axis_size("blk")
    local_rows, width = student.shape
    nz = groups // X_LO
    share_rows = local_rows // blks
    part_rows = share_rows // 2
    dist = nz // 2
    dma = pltpu.SemaphoreType.DMA
    pairs = groups * local_rows * 2 * groups * local_rows // (groups * blks)
    return pl.pallas_call(
        functools.partial(kernel, groups=groups, blks=blks),
        out_shape=jax.ShapeDtypeStruct((share_rows, width), jnp.float32),
        in_specs=[pl.BlockSpec(memory_space=pltpu.HBM)] * 2,
        out_specs=pl.BlockSpec(memory_space=pltpu.VMEM),
        scratch_shapes=[
            pltpu.VMEM((2 * local_rows, width), jnp.bfloat16),
            pltpu.VMEM((2 * local_rows // 256, 8, 256), jnp.float32),
            pltpu.VMEM((nz, 2, 2, part_rows, width), jnp.bfloat16),
            pltpu.VMEM((nz * 2 * share_rows, 128), jnp.float32),
            pltpu.VMEM((nz * 2 * share_rows, 128), jnp.float32),
            pltpu.VMEM((nz * 2 * share_rows, width), jnp.float32),
            pltpu.VMEM((nz, 2, part_rows, width), jnp.bfloat16),
            pltpu.VMEM((nz, 2, part_rows, width), jnp.bfloat16),
            pltpu.VMEM((2, dist - 1, 2, part_rows, width), jnp.bfloat16),
            pltpu.VMEM((2, dist - 1, 2, part_rows, width), jnp.bfloat16),
            pltpu.VMEM((2, part_rows, width), jnp.bfloat16),
            pltpu.VMEM((2, part_rows, width), jnp.bfloat16),
            dma((2,)),
            dma((2,)),
            dma((2, dist, 2)),
            dma((2, dist, 2)),
            dma((nz, 2)),
            dma((nz, 2)),
            dma((nz, 2)),
            dma((nz, 2)),
            dma((2, dist - 1, 2)),
            dma((2, dist - 1, 2)),
            dma((2,)),
            dma((2,)),
        ],
        compiler_params=pltpu.CompilerParams(
            collective_id=0, has_side_effects=True, vmem_limit_bytes=52 * 1024 * 1024
        ),
        cost_estimate=pl.CostEstimate(
            flops=4 * pairs * width, bytes_accessed=8 * 1024 * 1024, transcendentals=pairs
        ),
    )(student, teacher)


def solution(mesh):
    in_specs = (P("group", None), P("group", None))
    out_specs = P(("group", "blk"), None)
    return jax.shard_map(local, mesh=mesh, in_specs=in_specs, out_specs=out_specs, check_vma=False)
```

time: 355 us -> 54.5 us (0.15); the launches traced: 347 us -> 54.4 us
  waiting for transfers between devices: 286 us -> 0 us
  Pallas kernels: 0 us -> 53.7 us
  matrix products: 19.9 us -> 0 us
  other arithmetic: 15.4 us -> 0 us
  between operations: 13.2 us -> 0.01 us
  local copies, waits for them, and re-layouts: 13.1 us -> 0.71 us
    psum x1 -> x0, waiting for transfers between devices: 152 us -> none  [local(): totals = lax.psum(partial_value, 'blk')]
    all_gather x2 -> x0, waiting for transfers between devices: 133 us -> none  [the longest x1 72.5 us: local(): lax.all_gather(student_part, 'group', axis=0, tiled=True)]
    pallas_call x0 -> x1, Pallas kernels: none -> 53.7 us  [local(): pl.pallas_call(functools.partial(kernel, groups=groups, blks=blks), out_s...]
    dot_general x4 -> x0, matrix products: 19.9 us -> none  [the longest x2 12.6 us: cross(): lax.dot_general(left, right, (((1,), (1,)), ((), ())), preferred_element_...]
    reduce_sum x4 -> x0, other arithmetic: 11.4 us -> none  [the longest x3 6.2 us: squares(): return jnp.sum(wide * wide, axis=1)]
    add x1 -> x0, local copies, waits for them, and re-layouts: 5.35 us -> none  [pair_terms(): row_norm[:, None] + squares(student_cols)[None, :]]
    sub x1 -> x0, local copies, waits for them, and re-layouts: 5.34 us -> none  [pair_terms(): row_norm[:, None] + squares(teacher_cols)[None, :]]
  transfers between devices with their start and end apart: 3 -> 0, of which waited for: 3 -> 0; matrix products, arithmetic and copies ran while one was open for 4% -> 0% of each run, Pallas kernels for 0% -> 0%
where the time goes in v4:
time: 54.5 us; the launch traced here: 54.4 us
  Pallas kernels  53.7 us (99%)
  local copies, waits for them, and re-layouts  0.71 us (1%)
    pallas_call x1, Pallas kernels, local(): pl.pallas_call(functools.partial(kernel, groups=groups, blks=blks), out_s...  53.7 us

profile of v4, /device:TPU:8, one launch (start us, length us, event | category | flops | bytes accessed | tf_op | source)
XLA Modules:
  0.0 54.4 jit_solution(12313731170181054996)
XLA Ops:
  0.0 53.7 %shard_map.28 = f32[64,1024]{1,0:T(8,128)S(1)} custom-call(bf16[1024,1024]{1,0:T(8,128)(2,1)} %student.1, bf16[1024,1024]{1,0:T(8,128)(2,1)} %teacher.1), custom_call_target="tpu_custom_call" | custom-call | flops 8589934592 | bytes 8388608 | tf_op jit(solution)/shard_map/pallas_call | solution.py:322
  53.7 0.7 %copy.4 = f32[64,1024]{1,0:T(8,128)} copy(f32[64,1024]{1,0:T(8,128)S(1)} %shard_map.28) | data formatting | bytes 524288

commit v5 on v4

--- a/solution.py
+++ b/solution.py
@@ -11,6 +11,7 @@
 X_HI = 2
 X_LO = 2
 CORES = 2
+PARTS = 4
 X = X_HI * X_LO
 WIDEST = 8.0
 
@@ -34,13 +35,13 @@
     return jnp.where(wide < 0.0, -root, root)
 
 
-def kernel(student, teacher, out, cols, col_norm, rows, norm, mass, res, x_out, x_in, z_out, z_in, far_out, far_in,
+def kernel(student, teacher, out, cols, col_norm, rows, norm, mass, res, x_out, x_in, z_out, z_in,
            load_sem, own_sem, z_send, z_recv, x_send, x_recv,
-           x_back_send, x_back_recv, z_back_send, z_back_recv, far_send, far_recv, *, groups, blks):
+           x_back_send, x_back_recv, z_back_send, z_back_recv, *, groups, blks):
     nz = groups // X_LO
     width = cols.shape[1]
     part_rows = rows.shape[3]
-    share_rows = 2 * part_rows
+    share_rows = PARTS * part_rows
     local_rows = cols.shape[0] // 2
     half_nz = nz // 2
     last = nz - 1
@@ -85,6 +86,16 @@
             return last
         return 2 * dist - 1 + way
 
+    def side(part):
+        return part // (PARTS // 2)
+
+    def flip(part):
+        return (part + PARTS // 2) % PARTS
+
+    order = [
+        [(i % 2 ^ way) * (PARTS // 2) + i // 2 for i in range(PARTS)] for way in range(2)
+    ]
+
     def z_copy(way, dist, part):
         at = (way, dist - 1, part)
         src = own_part(part) if dist == 1 else rows.at[slot_of(way, dist - 1), 0, part]
@@ -96,17 +107,17 @@
         src = own_part(part) if slot == 0 else rows.at[slot, 0, part]
         at = (slot, part)
         return remote(
-            src, rows.at[slot, 1, 1 - part], x_send.at[at], x_recv.at[at], at_x(-1 if part == 0 else 1)
+            src, rows.at[slot, 1, flip(part)], x_send.at[at], x_recv.at[at], at_x(-1 if side(part) == 0 else 1)
         )
 
     def x_back(slot, index):
         at = (slot, index)
         return remote(
             x_out.at[at],
-            x_in.at[slot, 1 - index],
+            x_in.at[slot, flip(index)],
             x_back_send.at[at],
-            x_back_recv.at[slot, 1 - index],
-            at_x(1 if index == 1 else -1),
+            x_back_recv.at[slot, flip(index)],
+            at_x(1 if side(index) == 1 else -1),
         )
 
     def wait_x_back(slot, part):
@@ -119,11 +130,6 @@
         at = (way, dist - 1, part)
         return remote(
             z_out.at[at], z_in.at[at], z_back_send.at[at], z_back_recv.at[at], at_z(-away(way))
-        )
-
-    def far_back(part):
-        return remote(
-            far_out.at[part], far_in.at[part], far_send.at[part], far_recv.at[part], at_z(half_nz)
         )
 
     loads = [
@@ -132,10 +138,10 @@
     ]
     loads += [
         pltpu.make_async_copy(own_part(part), rows.at[0, 0, part], own_sem.at[part])
-        for part in range(2)
+        for part in range(PARTS)
     ]
     barrier = pltpu.get_barrier_semaphore()
-    partners = [at_z(1), at_z(-1), at_x(1), at_x(-1), at_z(half_nz)]
+    partners = [at_z(1), at_z(-1), at_x(1), at_x(-1)]
     for partner in partners:
         pl.semaphore_signal(barrier, inc=1, device_id=partner, device_id_type=pl.DeviceIdType.MESH)
     for copy in loads:
@@ -148,10 +154,10 @@
         copy.start()
         sent.append(copy)
 
-    for i in range(2):
+    for i in range(PARTS):
         for way in range(2):
-            send(z_copy(way, 1, (i + way) % 2))
-        send(x_copy(0, i))
+            send(z_copy(way, 1, order[way][i]))
+        send(x_copy(0, order[0][i]))
 
     rate = math.log2(math.e) / (WIDEST * width)
     for copy in loads:
@@ -192,9 +198,11 @@
         )
         return folded, pulled
 
-    def use(slot, count, quarters=range(4)):
-        row = rows[slot : slot + count].reshape(-1, width)
-        where = slice(slot * 2 * share_rows, (slot + count) * 2 * share_rows)
+    def use(slot, count, quarters=range(4), half=None):
+        read = rows[slot : slot + count] if half is None else rows[slot, half]
+        row = read.reshape(-1, width)
+        start = (2 * slot + (half or 0)) * share_rows
+        where = slice(start, start + row.shape[0])
         if 0 in quarters:
             wide = row.astype(jnp.float32)
             total = jnp.sum(wide * wide, axis=1, keepdims=True)
@@ -211,10 +219,12 @@
             diff = jnp.sum(mass[where, :], axis=1, keepdims=True)
             whole = res[where, :] - diff * row.astype(jnp.float32)
             res[where, :] = whole
+            if half == 0:
+                return
             for c in range(count):
-                for index in range(2):
-                    start = (2 * c + 1) * share_rows + index * part_rows
-                    x_out[slot + c, index] = encode(whole[start : start + part_rows])
+                for index in range(PARTS):
+                    begin = (2 * c + (half is None)) * share_rows + index * part_rows
+                    x_out[slot + c, index] = encode(whole[begin : begin + part_rows])
 
     def own_sum(slot, part):
         wait_x_back(slot, part)
@@ -229,85 +239,90 @@
         start = slot * 2 * share_rows + part * part_rows
         return res[start : start + part_rows, :]
 
-    def arrive(dist, i):
-        for way in range(2):
-            part = (i + way) % 2
-            z_copy(way, dist, part).wait_recv()
-            if dist + 1 < half_nz or (dist + 1 == half_nz and part == way):
-                send(z_copy(way, dist + 1, part))
-            send(x_copy(slot_of(way, dist), part))
+    def arrive(dist, indices):
+        for i in indices:
+            for way in range(2):
+                part = order[way][i]
+                if dist == half_nz and side(part) != way:
+                    continue
+                z_copy(way, dist, part).wait_recv()
+                if dist + 1 < half_nz or (dist + 1 == half_nz and side(part) == way):
+                    send(z_copy(way, dist + 1, part))
+                send(x_copy(slot_of(way, dist), part))
 
     def cross(*slots):
         for slot in slots:
-            for part in range(2):
+            for part in range(PARTS):
                 x_copy(slot, part).wait_recv()
 
     def give_back(*slots):
-        for slot in slots:
-            for index in range(2):
+        for index in range(PARTS):
+            for slot in slots:
                 send(x_back(slot, index))
 
-    arrive(1, 0)
-    arrive(1, 1)
-    cross(0)
-    use(0, 1)
-    for dist in range(2, half_nz):
-        slot = slot_of(0, dist - 1)
-        if dist == 2:
-            arrive(2, 0)
-            arrive(2, 1)
-        cross(slot, slot + 1)
-        use(slot, 2, range(2))
-        if dist + 1 < half_nz:
-            arrive(dist + 1, 0)
-        else:
-            arrive(half_nz, 0)
-            give_back(0)
-            for early in range(1, half_nz - 2):
-                give_back(slot_of(0, early), slot_of(1, early))
-        use(slot, 2, range(2, 4))
-        if dist + 1 < half_nz:
-            arrive(dist + 1, 1)
-    slot = slot_of(0, half_nz - 2)
-    give_back(slot, slot + 1)
-    slot = slot_of(0, half_nz - 1)
-    cross(slot, slot + 1)
-    use(slot, 2)
-    give_back(slot, slot + 1)
+    everything, first, second = range(PARTS), range(PARTS // 2), range(PARTS // 2, PARTS)
+    near, mid, far = (slot_of(0, dist) for dist in range(1, half_nz))
+    arrive(1, everything)
+    arrive(2, everything)
+    cross(near, near + 1)
+    use(near, 2, [0])
+    arrive(3, first)
+    use(near, 2, [1])
+    arrive(3, second)
+    cross(mid, mid + 1)
+    use(mid, 2, [0])
+    arrive(4, first)
+    use(mid, 2, [1])
+    arrive(4, second)
+    cross(far, far + 1)
+    use(far, 2)
+    give_back(far, far + 1)
     cross(last)
     use(last, 1)
     give_back(last)
-
-    for dist in range(half_nz - 1):
-        for slot in sorted({slot_of(0, dist), slot_of(1, dist)}):
-            for part in range(2):
-                keep(slot, part)
-    for part in range(2):
-        for way in range(2):
-            z_out[way, half_nz - 2, part] = encode(own_sum(slot_of(way, half_nz - 1), part))
-            send(z_back(way, half_nz - 1, part))
-    for part in range(2):
-        far_out[part] = encode(own_sum(last, part))
-        send(far_back(part))
-    for dist in range(half_nz - 2, 0, -1):
-        for part in range(2):
-            for way in range(2):
+    cross(0)
+
+    def hand_back(way, dist, part, total):
+        z_out[way, dist - 1, part] = encode(total)
+        send(z_back(way, dist, part))
+
+    def both(parts):
+        return [(way, part) for i in range(PARTS // 2) for way in range(2) for part in [parts(way)[i]]]
+
+    ready = both(lambda way: [part for part in everything if side(part) != way])
+    later = both(lambda way: [part for part in everything if side(part) == way])
+    for way, part in ready:
+        hand_back(way, half_nz - 1, part, own_sum(slot_of(way, half_nz - 1), part))
+    for way, part in later:
+        hand_back(way, half_nz, part, own_sum(last, part))
+    use(mid, 2, [2, 3])
+    give_back(mid, mid + 1)
+    for way, part in later:
+        keep(slot_of(way, half_nz - 1), part)
+    for way, part in later:
+        z_back(way, half_nz, part).wait_recv()
+        total = kept(slot_of(way, half_nz - 1), part) + decode(z_in[way, half_nz - 1, part])
+        hand_back(way, half_nz - 1, part, total)
+    use(near, 2, [2, 3])
+    give_back(near, near + 1)
+    for dist in range(half_nz - 2, -1, -1):
+        for way, part in ready + later if dist else [(0, part) for part in everything]:
+            keep(slot_of(way, dist), part)
+        if dist > 0:
+            for way, part in ready + later:
                 z_back(way, dist + 1, part).wait_recv()
-                z_out[way, dist - 1, part] = encode(
-                    kept(slot_of(way, dist), part) + decode(z_in[way, dist, part])
-                )
-                send(z_back(way, dist, part))
-    for part in range(2):
-        far_back(part).wait_recv()
-        res[part * part_rows : (part + 1) * part_rows, :] = kept(0, part) + decode(far_in[part])
+                hand_back(way, dist, part, kept(slot_of(way, dist), part) + decode(z_in[way, dist, part]))
+        if dist + 2 == half_nz:
+            use(0, 1)
+            give_back(0)
     for copy in sent:
         copy.wait_send()
-    for part in range(2):
-        total = kept(0, part)
-        for way in range(2):
+    scale = 1.0 / (groups * local_rows)
+    for pick in (ready, later):
+        for way, part in pick:
             z_back(way, 1, part).wait_recv()
-            total = total + decode(z_in[way, 0, part])
-        out[part * part_rows : (part + 1) * part_rows, :] = total * (1.0 / (groups * local_rows))
+            res[part * part_rows : (part + 1) * part_rows, :] = kept(0, part) + decode(z_in[way, 0, part])
+    out[...] = res[:share_rows, :] * scale
 
 
 def local(student, teacher):
@@ -315,7 +330,7 @@
     local_rows, width = student.shape
     nz = groups // X_LO
     share_rows = local_rows // blks
-    part_rows = share_rows // 2
+    part_rows = share_rows // PARTS
     dist = nz // 2
     dma = pltpu.SemaphoreType.DMA
     pairs = groups * local_rows * 2 * groups * local_rows // (groups * blks)
@@ -327,28 +342,24 @@
         scratch_shapes=[
             pltpu.VMEM((2 * local_rows, width), jnp.bfloat16),
             pltpu.VMEM((2 * local_rows // 256, 8, 256), jnp.float32),
-            pltpu.VMEM((nz, 2, 2, part_rows, width), jnp.bfloat16),
+            pltpu.VMEM((nz, 2, PARTS, part_rows, width), jnp.bfloat16),
             pltpu.VMEM((nz * 2 * share_rows, 128), jnp.float32),
             pltpu.VMEM((nz * 2 * share_rows, 128), jnp.float32),
             pltpu.VMEM((nz * 2 * share_rows, width), jnp.float32),
-            pltpu.VMEM((nz, 2, part_rows, width), jnp.bfloat16),
-            pltpu.VMEM((nz, 2, part_rows, width), jnp.bfloat16),
-            pltpu.VMEM((2, dist - 1, 2, part_rows, width), jnp.bfloat16),
-            pltpu.VMEM((2, dist - 1, 2, part_rows, width), jnp.bfloat16),
-            pltpu.VMEM((2, part_rows, width), jnp.bfloat16),
-            pltpu.VMEM((2, part_rows, width), jnp.bfloat16),
+            pltpu.VMEM((nz, PARTS, part_rows, width), jnp.bfloat16),
+            pltpu.VMEM((nz, PARTS, part_rows, width), jnp.bfloat16),
+            pltpu.VMEM((2, dist, PARTS, part_rows, width), jnp.bfloat16),
+            pltpu.VMEM((2, dist, PARTS, part_rows, width), jnp.bfloat16),
             dma((2,)),
-            dma((2,)),
-            dma((2, dist, 2)),
-            dma((2, dist, 2)),
-            dma((nz, 2)),
-            dma((nz, 2)),
-            dma((nz, 2)),
-            dma((nz, 2)),
-            dma((2, dist - 1, 2)),
-            dma((2, dist - 1, 2)),
-            dma((2,)),
-            dma((2,)),
+            dma((PARTS,)),
+            dma((2, dist, PARTS)),
+            dma((2, dist, PARTS)),
+            dma((nz, PARTS)),
+            dma((nz, PARTS)),
+            dma((nz, PARTS)),
+            dma((nz, PARTS)),
+            dma((2, dist, PARTS)),
+            dma((2, dist, PARTS)),
         ],
         compiler_params=pltpu.CompilerParams(
             collective_id=0, has_side_effects=True, vmem_limit_bytes=52 * 1024 * 1024

time: 54.5 us -> 51.2 us (0.939)
  Pallas kernels: 53.7 us -> 50.4 us
    pallas_call x1, Pallas kernels: 53.7 us -> 50.4 us  [local(): pl.pallas_call(functools.partial(kernel, groups=groups, blks=blks), out_s...]
where the time goes in v5:
time: 51.2 us; the launch traced here: 51.1 us
  Pallas kernels  50.4 us (98%)
  local copies, waits for them, and re-layouts  0.71 us (1%)
    pallas_call x1, Pallas kernels, local(): pl.pallas_call(functools.partial(kernel, groups=groups, blks=blks), out_s...  50.4 us

profile of v5, /device:TPU:8, one launch (start us, length us, event | category | flops | bytes accessed | tf_op | source)
XLA Modules:
  0.0 51.1 jit_solution(3312114603764115891)
XLA Ops:
  0.0 50.4 %shard_map.28 = f32[64,1024]{1,0:T(8,128)S(1)} custom-call(bf16[1024,1024]{1,0:T(8,128)(2,1)} %student.1, bf16[1024,1024]{1,0:T(8,128)(2,1)} %teacher.1), custom_call_target="tpu_custom_call" | custom-call | flops 8589934592 | bytes 8388608 | tf_op jit(solution)/shard_map/pallas_call | solution.py:337
  50.4 0.7 %copy.4 = f32[64,1024]{1,0:T(8,128)} copy(f32[64,1024]{1,0:T(8,128)S(1)} %shard_map.28) | data formatting | bytes 524288

commit v6 on v5

--- a/solution.py
+++ b/solution.py
@@ -92,9 +92,7 @@
     def flip(part):
         return (part + PARTS // 2) % PARTS
 
-    order = [
-        [(i % 2 ^ way) * (PARTS // 2) + i // 2 for i in range(PARTS)] for way in range(2)
-    ]
+    order = [[(way * (PARTS // 2) + i) % PARTS for i in range(PARTS)] for way in range(2)]
 
     def z_copy(way, dist, part):
         at = (way, dist - 1, part)
@@ -157,7 +155,7 @@
     for i in range(PARTS):
         for way in range(2):
             send(z_copy(way, 1, order[way][i]))
-        send(x_copy(0, order[0][i]))
+        send(x_copy(0, (i % 2) * (PARTS // 2) + i // 2))
 
     rate = math.log2(math.e) / (WIDEST * width)
     for copy in loads:
@@ -193,10 +191,7 @@
             weights.append(weight)
             wide = weight.astype(jnp.float32)
             folded = wide if folded is None else folded + wide
-        pulled = jnp.dot(
-            jnp.concatenate(weights, axis=1), col, preferred_element_type=jnp.float32
-        )
-        return folded, pulled
+        return folded, weights
 
     def use(slot, count, quarters=range(4), half=None):
         read = rows[slot : slot + count] if half is None else rows[slot, half]
@@ -207,14 +202,22 @@
             wide = row.astype(jnp.float32)
             total = jnp.sum(wide * wide, axis=1, keepdims=True)
             norm[where, :] = jnp.broadcast_to(0.125 - rate * total, (row.shape[0], 128))
+        folded, weights = None, []
         for quarter in quarters:
-            folded, pulled = weigh(row, norm[where, :], quarter * step)
-            if quarter == 0:
-                mass[where, :] = folded
-                res[where, :] = pulled
-            else:
-                mass[where, :] += folded
-                res[where, :] += pulled
+            more, weight = weigh(row, norm[where, :], quarter * step)
+            folded = more if folded is None else folded + more
+            weights += weight
+        pulled = jnp.dot(
+            jnp.concatenate(weights, axis=1),
+            cols[quarters[0] * step : (quarters[-1] + 1) * step, :],
+            preferred_element_type=jnp.float32,
+        )
+        if 0 in quarters:
+            mass[where, :] = folded
+            res[where, :] = pulled
+        else:
+            mass[where, :] += folded
+            res[where, :] += pulled
         if 3 in quarters:
             diff = jnp.sum(mass[where, :], axis=1, keepdims=True)
             whole = res[where, :] - diff * row.astype(jnp.float32)
@@ -273,7 +276,6 @@
     use(mid, 2, [0])
     arrive(4, first)
     use(mid, 2, [1])
-    arrive(4, second)
     cross(far, far + 1)
     use(far, 2)
     give_back(far, far + 1)

time: 51.2 us -> 50.1 us (0.979)
  Pallas kernels: 50.4 us -> 49.3 us
    pallas_call x1, Pallas kernels: 50.4 us -> 49.3 us  [local(): pl.pallas_call(functools.partial(kernel, groups=groups, blks=blks), out_s...]
where the time goes in v6:
time: 50.1 us; the launch traced here: 50 us
  Pallas kernels  49.3 us (98%)
  local copies, waits for them, and re-layouts  0.71 us (1%)
    pallas_call x1, Pallas kernels, local(): pl.pallas_call(functools.partial(kernel, groups=groups, blks=blks), out_s...  49.3 us

profile of v6, /device:TPU:8, one launch (start us, length us, event | category | flops | bytes accessed | tf_op | source)
XLA Modules:
  0.0 50.0 jit_solution(15981200176078079133)
XLA Ops:
  0.0 49.3 %shard_map.28 = f32[64,1024]{1,0:T(8,128)S(1)} custom-call(bf16[1024,1024]{1,0:T(8,128)(2,1)} %student.1, bf16[1024,1024]{1,0:T(8,128)(2,1)} %teacher.1), custom_call_target="tpu_custom_call" | custom-call | flops 8589934592 | bytes 8388608 | tf_op jit(solution)/shard_map/pallas_call | solution.py:339
  49.3 0.7 %copy.4 = f32[64,1024]{1,0:T(8,128)} copy(f32[64,1024]{1,0:T(8,128)S(1)} %shard_map.28) | data formatting | bytes 524288

commit v7 on v6

--- a/solution.py
+++ b/solution.py
@@ -55,10 +55,10 @@
     def at_z(step):
         return {"group": x_lo * nz + lax.rem(z + step + nz, nz), "blk": blk}
 
-    def at_x(step):
+    def at_x(step, z_step=0):
         to = lax.rem(x + step + X, X)
         return {
-            "group": lax.rem(to, X_LO) * nz + z,
+            "group": lax.rem(to, X_LO) * nz + lax.rem(z + z_step + nz, nz),
             "blk": (y * X_HI + to // X_LO) * CORES + core,
         }
 
@@ -110,12 +110,13 @@
 
     def x_back(slot, index):
         at = (slot, index)
+        way_home = 1 if side(index) == 1 else -1
         return remote(
             x_out.at[at],
             x_in.at[slot, flip(index)],
             x_back_send.at[at],
             x_back_recv.at[slot, flip(index)],
-            at_x(1 if side(index) == 1 else -1),
+            at_x(way_home, -way_home if slot == last else 0),
         )
 
     def wait_x_back(slot, part):
@@ -275,7 +276,8 @@
     cross(mid, mid + 1)
     use(mid, 2, [0])
     arrive(4, first)
-    use(mid, 2, [1])
+    use(mid, 2, [1, 2, 3])
+    give_back(mid, mid + 1)
     cross(far, far + 1)
     use(far, 2)
     give_back(far, far + 1)
@@ -293,17 +295,17 @@
 
     ready = both(lambda way: [part for part in everything if side(part) != way])
     later = both(lambda way: [part for part in everything if side(part) == way])
+    for way, part in later:
+        hand_back(way, half_nz, part, kept(last, part))
     for way, part in ready:
         hand_back(way, half_nz - 1, part, own_sum(slot_of(way, half_nz - 1), part))
-    for way, part in later:
-        hand_back(way, half_nz, part, own_sum(last, part))
-    use(mid, 2, [2, 3])
-    give_back(mid, mid + 1)
     for way, part in later:
         keep(slot_of(way, half_nz - 1), part)
     for way, part in later:
         z_back(way, half_nz, part).wait_recv()
-        total = kept(slot_of(way, half_nz - 1), part) + decode(z_in[way, half_nz - 1, part])
+        wait_x_back(last, part)
+        total = kept(slot_of(way, half_nz - 1), part) + decode(x_in[last, part])
+        total = total + decode(z_in[way, half_nz - 1, part])
         hand_back(way, half_nz - 1, part, total)
     use(near, 2, [2, 3])
     give_back(near, near + 1)

time: 50.1 us -> 49 us (0.978)
  Pallas kernels: 49.3 us -> 48.2 us
    pallas_call x1, Pallas kernels: 49.3 us -> 48.2 us  [local(): pl.pallas_call(functools.partial(kernel, groups=groups, blks=blks), out_s...]
where the time goes in v7:
time: 49 us; the launch traced here: 48.9 us
  Pallas kernels  48.2 us (98%)
  local copies, waits for them, and re-layouts  0.71 us (1%)
    pallas_call x1, Pallas kernels, local(): pl.pallas_call(functools.partial(kernel, groups=groups, blks=blks), out_s...  48.2 us

profile of v7, /device:TPU:8, one launch (start us, length us, event | category | flops | bytes accessed | tf_op | source)
XLA Modules:
  0.0 48.9 jit_solution(16200778799754591359)
XLA Ops:
  0.0 48.2 %shard_map.28 = f32[64,1024]{1,0:T(8,128)S(1)} custom-call(bf16[1024,1024]{1,0:T(8,128)(2,1)} %student.1, bf16[1024,1024]{1,0:T(8,128)(2,1)} %teacher.1), custom_call_target="tpu_custom_call" | custom-call | flops 8589934592 | bytes 8388608 | tf_op jit(solution)/shard_map/pallas_call | solution.py:341
  48.2 0.7 %copy.4 = f32[64,1024]{1,0:T(8,128)} copy(f32[64,1024]{1,0:T(8,128)S(1)} %shard_map.28) | data formatting | bytes 524288

commit v8 on v7

--- a/solution.py
+++ b/solution.py
@@ -276,8 +276,7 @@
     cross(mid, mid + 1)
     use(mid, 2, [0])
     arrive(4, first)
-    use(mid, 2, [1, 2, 3])
-    give_back(mid, mid + 1)
+    use(mid, 2, [1])
     cross(far, far + 1)
     use(far, 2)
     give_back(far, far + 1)
@@ -299,6 +298,8 @@
         hand_back(way, half_nz, part, kept(last, part))
     for way, part in ready:
         hand_back(way, half_nz - 1, part, own_sum(slot_of(way, half_nz - 1), part))
+    use(mid, 2, [2, 3])
+    give_back(mid, mid + 1)
     for way, part in later:
         keep(slot_of(way, half_nz - 1), part)
     for way, part in later:

time: 49 us -> 48.6 us (level)
  no operation moved by 1% of the time
where the time goes in v8:
time: 48.6 us; the launch traced here: 48.5 us
  Pallas kernels  47.8 us (98%)
  local copies, waits for them, and re-layouts  0.71 us (1%)
    pallas_call x1, Pallas kernels, local(): pl.pallas_call(functools.partial(kernel, groups=groups, blks=blks), out_s...  47.8 us

profile of v8, /device:TPU:8, one launch (start us, length us, event | category | flops | bytes accessed | tf_op | source)
XLA Modules:
  0.0 48.5 jit_solution(2298105101679828711)
XLA Ops:
  0.0 47.8 %shard_map.28 = f32[64,1024]{1,0:T(8,128)S(1)} custom-call(bf16[1024,1024]{1,0:T(8,128)(2,1)} %student.1, bf16[1024,1024]{1,0:T(8,128)(2,1)} %teacher.1), custom_call_target="tpu_custom_call" | custom-call | flops 8589934592 | bytes 8388608 | tf_op jit(solution)/shard_map/pallas_call | solution.py:342
  47.8 0.7 %copy.4 = f32[64,1024]{1,0:T(8,128)} copy(f32[64,1024]{1,0:T(8,128)S(1)} %shard_map.28) | data formatting | bytes 524288
